TPU v7x, 128 devices: a whole 4x4x4 slice. The times are simulated.
128 devices in a mesh: row: 16 (over y, x), col: 8 (over z, core).
Axes of the slice: x: 4, y: 4, z: 4, core: 2. Of those that a mesh axis runs over, the one named last changes fastest.
Arguments:
- band_tiles: bfloat16 [16, 128, 256, 256], P('row', 'col'), may hold values from 0.0009994507 to 1
- band_cell: int32 [16, 128], P('row', 'col'), may hold values from 0 to 31, as said below
- band_count: int32 [16, 8], P('row', 'col'), may hold values from 1 to 16, as said below
- matrix_tiles: bfloat16 [16, 64, 256, 256], P('row', 'col'), may hold values from 7.390976e-05 to 0.07421875
- matrix_col: int32 [16, 64], P('row', 'col'), may hold values from 0 to 15
- matrix_live: int32 [16, 64], P('row', 'col'), may hold values 0 or 1
Outputs:
- reached: bfloat16 [8192, 32768], P('row', 'col')
- gained: float32 [], replicated
Inputs may be any that keep to these rules, and one draw needn't show every extreme that they name: The band_cell values of one device's 16 slots are distinct. `band_count`: among the 8 devices of one index of row, the live slots with slot number 16 // 2 or more number at most 8 in all.
All inputs are finite; a program needn't handle non-finite values. No bound on the sum of `matrix_live` on one device may be relied on, other than what follows from the above.
Results may differ from a plain program's by a relative error of at most 0.001.
Values may be sent and summed in bfloat16 or wider, within the bound.
A program may use at most 128 MiB of HBM per device.

v0:
```python
import jax
import jax.numpy as jnp
from jax import lax
from jax.sharding import Mesh
from jax.sharding import PartitionSpec as P

TILES = 128
BR = 2
COL = ("col_0", "col_1")
ROW = ("row_0", "row_1")
ROW_COL = ("row_0", "row_1", "col_0", "col_1")


def rows_for(lines, length):
    spare = -lines.shape[0] % length
    if not spare:
        return lines
    return jnp.concatenate([lines, jnp.zeros((spare, *lines.shape[1:]), lines.dtype)])


def sum_by_parts(shard, axis):
    lines = shard.reshape(-1, *shard.shape[1:][-1:])
    own = lax.psum_scatter(
        rows_for(lines, lax.axis_size(axis)), axis, scatter_dimension=0, tiled=True
    )
    whole = lax.all_gather(own, axis).reshape(-1, *lines.shape[1:])
    return lax.slice_in_dim(whole, 0, len(lines)).reshape(shard.shape)


def over_axes(shard, axes):
    for axis in axes:
        shard = lax.psum(shard, axis)
    return shard


def on_device(band_tiles, band_cell, band_count, matrix_tiles, matrix_col, matrix_live):
    slots_own = band_tiles.shape[1]
    tile = band_tiles.shape[-1]
    n_col = lax.axis_size(COL)
    tcols = TILES // n_col
    places = BR * tcols
    spots = jnp.arange(places, dtype=jnp.int32)
    b_tiles, b_index, b_live = (
        lax.all_gather(matrix_tiles, ROW, axis=0, tiled=True),
        lax.all_gather(matrix_col, ROW, axis=0, tiled=True),
        lax.all_gather(matrix_live, ROW, axis=0, tiled=True),
    )
    flat_tiles = b_tiles.reshape(-1, tile, tile)
    half = slots_own // 2
    front_tiles, a_cell, a_count = (
        lax.all_gather(band_tiles[:, :half], COL, axis=1, tiled=True),
        lax.all_gather(band_cell, COL, axis=1, tiled=True),
        lax.all_gather(band_count, COL, axis=1, tiled=True),
    )
    counts = a_count[0]
    spill = jnp.maximum(counts - half, 0)
    before = jnp.cumsum(spill) - spill
    ending = before + spill
    mine = lax.axis_index(COL)
    own_before = jnp.take(before, mine)
    own_spill = jnp.maximum(band_count[0, 0] - half, 0)
    pack_spot = jnp.arange(half, dtype=jnp.int32)
    upper = jnp.arange(half, dtype=jnp.int32)
    place_w = (
        (pack_spot[:, None] == own_before + upper[None, :]) & (upper[None, :] < own_spill)
    ).astype(jnp.bfloat16)
    packed = jnp.einsum(
        "qs,sxy->qxy", place_w, band_tiles[0, half:], preferred_element_type=jnp.float32
    )
    spilled = (
        sum_by_parts(packed.astype(jnp.bfloat16), COL).astype(jnp.float32).astype(jnp.bfloat16)
    )
    holder = jnp.sum((ending[None, :] <= pack_spot[:, None]).astype(jnp.int32), axis=1)
    holder = jnp.clip(holder, 0, n_col - 1)
    spill_slot = jnp.clip(half + pack_spot - jnp.take(before, holder), 0, slots_own - 1)
    spill_cell = jnp.take(a_cell[0], holder * slots_own + spill_slot)
    spill_valid = pack_spot < jnp.sum(spill)
    front = jnp.arange(n_col * half, dtype=jnp.int32)
    front_source = front // half
    front_slot = front % half
    front_cell = jnp.take(a_cell[0], front_source * slots_own + front_slot)
    front_valid = front_slot < jnp.take(counts, front_source)
    sources = jnp.concatenate([front_source, holder])
    cells = jnp.concatenate([front_cell, spill_cell])
    valid = jnp.concatenate([front_valid, spill_valid])
    tiles = jnp.concatenate([front_tiles[0], spilled], axis=0)
    k_glob = sources * tcols + cells % tcols
    i_loc = cells // tcols
    picked = jnp.take(flat_tiles, k_glob, axis=0)
    picked_index = jnp.take(b_index.reshape(-1), k_glob)
    picked_live = jnp.take(b_live.reshape(-1), k_glob)
    live = (picked_live > 0) & valid
    position = i_loc * tcols + picked_index
    product = jnp.einsum("axy,ayz->axz", tiles, picked, preferred_element_type=jnp.float32)
    weights = ((position[:, None] == spots[None, :]) & live[:, None]).astype(jnp.float32)
    summed = jnp.einsum("ap,axz->pxz", weights, product, precision=lax.Precision.HIGHEST)
    own_live = jnp.arange(slots_own, dtype=jnp.int32) < band_count[0, 0]
    own_w = ((band_cell[0][:, None] == spots[None, :]) & own_live[:, None]).astype(jnp.bfloat16)
    base = jnp.einsum("sp,sxz->pxz", own_w, band_tiles[0], preferred_element_type=jnp.float32)
    expanded = jnp.minimum(1.0, base + summed)
    block = (
        expanded.reshape(BR, tcols, tile, tile)
        .transpose(0, 2, 1, 3)
        .reshape(BR * tile, tcols * tile)
    )
    total = over_axes(jnp.sum(expanded - base), ROW_COL)
    devices = lax.axis_size(ROW) * n_col
    gained = total / (tile * tile * devices * places)
    return (block.astype(jnp.bfloat16), gained)


def solution(mesh):
    split = Mesh(mesh.devices.reshape(4, 4, 4, 2), ("row_0", "row_1", "col_0", "col_1"))
    placed = (
        P(ROW, COL, None, None),
        P(ROW, COL),
        P(ROW, COL),
        P(ROW, COL, None, None),
        P(ROW, COL),
        P(ROW, COL),
    )
    return jax.shard_map(
        on_device, mesh=split, in_specs=placed, out_specs=(P(ROW, COL), P()), check_vma=False
    )
```

profile of v0, /device:TPU:1, one launch (start us, length us, event | category | flops | bytes accessed | tf_op | source)
XLA Modules:
  0.0 311.7 jit_solution(18201135137651149009)
XLA Ops:
  8.9 1.2 dynamic-slice.3
  10.8 0.7 bitcast_dynamic-update-slice_fusion
  11.5 0.8 bitcast_dynamic-update-slice_fusion.1
  12.2 9.8 %all-reduce.2 = (s32[8]{0:T(128)S(1)}, s32[128]{0:T(128)S(1)}) all-reduce(s32[8]{0:T(128)S(1)} %bitcast_dynamic-update-slice_fusion, s32[128]{0:T(128)S(1)} %bitcast_dynamic-update-slice_fusion.1), channel_id=1, replica_groups=mesh['row_0'=4,'row_1'=4,'col_0'=4,'col_1'=2] {'col_0','col_1'}, use_global_device_ids=true, to_apply=%add.1 | all-reduce | flops 136 | bytes 1088
  22.0 0.6 fusion.42
  22.6 0.2 reduce-window.8
  22.8 0.6 dynamic-slice.2
  24.1 1.3 slice.7
  25.4 0.7 convolution_convert_fusion
  26.1 1.2 copy.24
  27.3 0.0 all-gather.9.cloned.1.call-start
  27.3 0.5 all-gather.9.cloned.1.call-update
  27.9 29.4 %reduce-scatter.2.cloned.1.call-done = bf16[256,256]{1,0:T(8,128)(2,1)} async-done(((bf16[2048,256]{1,0:T(8,128)(2,1)}), bf16[256,256]{1,0:T(8,128)(2,1)}) %reduce-scatter.2.cloned.1.call-update) | async-done | bytes 131088 | tf_op jit(solution)/shard_map/reduce_scatter | solution.py:23
  57.3 0.0 all-gather.7.cloned.1.call-start
  57.4 1.0 slice.43
  58.4 0.1 convert_reduce_fusion
  58.6 0.6 gather_fusion.1
  59.3 0.6 gather_fusion.2
  59.9 0.8 gather_fusion
  60.7 17.2 %all-gather.1 = s32[16,1,8]{2,1,0:T(1,128)S(1)} all-gather(s32[1,1,8]{2,1,0:T(1,128)S(1)} %bitcast.102), channel_id=1, replica_groups=mesh['row_0'=4,'row_1'=4,'col_0'=4,'col_1'=2] {'row_0','row_1'}, dimensions={0}, use_global_device_ids=true | all-gather | bytes 544 | tf_op jit(solution)/shard_map/all_gather | solution.py:45
  77.9 0.5 broadcast.1065
  78.4 0.7 reduce.7
  79.1 0.1 reshape.382
  79.2 17.3 %all-gather.2 = s32[16,1,8]{2,1,0:T(1,128)S(1)} all-gather(s32[1,1,8]{2,1,0:T(1,128)S(1)} %bitcast.103), channel_id=1, replica_groups=mesh['row_0'=4,'row_1'=4,'col_0'=4,'col_1'=2] {'row_0','row_1'}, dimensions={0}, use_global_device_ids=true | all-gather | bytes 544 | tf_op jit(solution)/shard_map/all_gather | solution.py:46
  96.5 0.7 reduce.8
  97.1 0.1 reshape.383
  97.3 0.1 compare_and_fusion
  97.4 1.2 gather_fusion.4
  98.6 1.2 gather_fusion.5
  99.9 0.6 iota_compare_fusion.5
  100.4 0.1 fusion.37
  100.5 0.7 fusion.45
  101.2 5.0 %fusion.32 = pred[64]{0:T(512)(128)(4,1)S(1)} fusion(s32[]{:T(128)} %bitcast.20, s32[]{:T(128)} %bitcast.21, s32[]{:T(128)} %bitcast.22, s32[]{:T(128)} %bitcast.23, s32[]{:T(128)} %bitcast.24, s32[]{:T(128)} %bitcast.26, s32[]{:T(128)} %bitcast.25, s32[]{:T(128)} %bitcast.19), kind=kLoop, calls=%fused_computation.91 | loop fusion | flops 2880 | bytes 96 | tf_op jit(solution)/shard_map/lt | solution.py:82
  106.2 0.1 select_add_fusion
  106.3 0.1 add_and_fusion
  106.4 35.1 %all-gather.9.cloned.1.call-done = bf16[16,8,256,256]{3,2,1,0:T(8,128)(2,1)} async-done(((bf16[1,8,256,256]{3,2,1,0:T(8,128)(2,1)}), bf16[16,8,256,256]{3,2,1,0:T(8,128)(2,1)}) %all-gather.9.cloned.1.call-update) | async-done | bytes 16777232 | tf_op jit(solution)/shard_map/all_gather | solution.py:44
  141.5 11.8 %gather_fusion.3 = bf16[72,256,256]{2,1,0:T(8,128)(2,1)} fusion(bf16[128,256,256]{2,1,0:T(8,128)(2,1)} %bitcast.96, s32[1024]{0:T(1024)S(1)} %pad_clamp_fusion), kind=kCustom, calls=%fused_computation.5 | custom fusion | bytes 18874656 | tf_op jit(solution)/shard_map/jit(_take)/gather | solution.py:89
  153.3 13.3 %all-gather.11.cloned.1.call-done = bf16[2048,256]{1,0:T(8,128)(2,1)} async-done(((bf16[256,256]{1,0:T(8,128)(2,1)}), bf16[2048,256]{1,0:T(8,128)(2,1)}) %all-gather.11.cloned.1.call-update) | async-done | bytes 1048592 | tf_op jit(solution)/shard_map/all_gather | solution.py:26
  166.6 51.8 %all-gather.7.cloned.1.call-done = bf16[1,64,256,256]{3,2,0,1:T(8,128)(2,1)} async-done(((bf16[1,8,256,256]{3,2,0,1:T(8,128)(2,1)}), bf16[1,64,256,256]{3,2,0,1:T(8,128)(2,1)}) %all-gather.7.cloned.1.call-update) | async-done | bytes 8388624 | tf_op jit(solution)/shard_map/all_gather | solution.py:51
  218.4 13.5 %fusion.2 = f32[72,256,256]{2,1,0:T(8,128)} fusion(bf16[8,256,256]{2,1,0:T(8,128)(2,1)} %bitcast.105, bf16[64,256,256]{2,1,0:T(8,128)(2,1)} %bitcast.104, bf16[72,256,256]{2,1,0:T(8,128)(2,1)} %gather_fusion.3, pred[72]{0:T(512)(128)(4,1)S(1)} %get-tuple-element.16), kind=kOutput, calls=%fused_computation.8 | convolution fusion | flops 2425356288 | bytes 37748808 | tf_op jit(solution)/shard_map/axy,ayz->axz/dot_general | solution.py:94
  231.9 24.1 %fusion = f32[32,256,256]{2,0,1:T(8,128)S(1)} fusion(f32[72,256,256]{2,1,0:T(8,128)} %fusion.2, s32[72]{0:T(128)S(1)} %select_add_fusion, pred[72]{0:T(512)(128)(4,1)S(1)} %add_and_fusion), kind=kOutput, calls=%fused_computation.6 | convolution fusion | flops 1811943936 | bytes 27263336 | tf_op jit(solution)/shard_map/ap,axz->pxz/dot_general | solution.py:96
  256.0 5.2 %subtract_reduce_fusion = (f32[]{:T(128)}, bf16[32,256,256]{2,0,1:T(8,128)(2,1)}) fusion(f32[32,256,256]{2,0,1:T(8,128)S(1)} %fusion, bf16[16,256,256]{2,1,0:T(8,128)(2,1)S(1)} %bitcast.95, s32[16]{0:T(128)S(1)} %bitcast.101, pred[16]{0:T(512)(128)(4,1)S(1)} %iota_compare_fusion.6), kind=kOutput, calls=%fused_computation.14 | convolution fusion | flops 77595648 | bytes 14680148 | tf_op jit(solution)/shard_map/sp,sxz->pxz/dot_general | solution.py:99
  261.2 9.0 %psum.28 = f32[]{:T(128)} all-reduce(f32[]{:T(128)} %get-tuple-element.18), channel_id=1, replica_groups=mesh['row_0'=4,'row_1'=4,'col_0'=4,'col_1'=2] {'row_0'}, use_global_device_ids=true, to_apply=%region_5.7 | all-reduce | flops 1 | bytes 8 | tf_op jit(solution)/shard_map/psum | solution.py:32
  270.3 9.0 %psum.29 = f32[]{:T(128)} all-reduce(f32[]{:T(128)} %psum.28), channel_id=1, replica_groups=mesh['row_0'=4,'row_1'=4,'col_0'=4,'col_1'=2] {'row_1'}, use_global_device_ids=true, to_apply=%region_6.8 | all-reduce | flops 1 | bytes 8 | tf_op jit(solution)/shard_map/psum | solution.py:32
  279.3 7.1 %psum.30 = f32[]{:T(128)} all-reduce(f32[]{:T(128)} %psum.29), channel_id=1, replica_groups=mesh['row_0'=4,'row_1'=4,'col_0'=4,'col_1'=2] {'col_0'}, use_global_device_ids=true, to_apply=%region_7.9 | all-reduce | flops 1 | bytes 8 | tf_op jit(solution)/shard_map/psum | solution.py:32
  286.4 9.3 %psum.31 = f32[]{:T(128)} all-reduce(f32[]{:T(128)} %psum.30), channel_id=1, replica_groups=mesh['row_0'=4,'row_1'=4,'col_0'=4,'col_1'=2] {'col_1'}, use_global_device_ids=true, to_apply=%region_8.10 | all-reduce | flops 1 | bytes 8 | tf_op jit(solution)/shard_map/psum | solution.py:32
  295.6 2.5 copy.26
  298.1 4.2 %copy.28 = bf16[64,8,16,256]{3,1,2,0:T(8,128)(2,1)} copy(bf16[64,8,16,256]{3,2,1,0:T(8,128)(2,1)S(1)} %bitcast.93) | data formatting | bytes 8388608
  (32 shorter events, 0.3 us)
Async XLA Ops:
  8.0 49.4 %copy-start = (bf16[1,16,256,256]{3,2,1,0:T(8,128)(2,1)S(1)}, bf16[1,16,256,256]{3,2,1,0:T(8,128)(2,1)}, u32[]{:S(2)}) copy-start(bf16[1,16,256,256]{3,2,1,0:T(8,128)(2,1)} %param.8) | copy-start | bytes 6291460
  8.0 52.7 %copy-start.2 = (s32[1,8]{1,0:T(1,128)S(1)}, s32[1,8]{1,0:T(1,128)}, u32[]{:S(2)}) copy-start(s32[1,8]{1,0:T(1,128)} %param.12) | copy-start | bytes 100
  8.0 71.2 %copy-start.3 = (s32[1,8]{1,0:T(1,128)S(1)}, s32[1,8]{1,0:T(1,128)}, u32[]{:S(2)}) copy-start(s32[1,8]{1,0:T(1,128)} %param.13) | copy-start | bytes 100
  8.0 49.3 %reduce-scatter.2.cloned.1.call-start = ((), (), s32[]{:S(2)}) async-start(), calls=%async_computation.2 | async-start | bytes 1179648 | tf_op jit(solution)/shard_map/reduce_scatter | solution.py:23
  27.3 114.2 %all-gather.9.cloned.1.call-start = ((), (), s32[]{:S(2)}) async-start(), calls=%async_computation.3 | async-start | bytes 17825792 | tf_op jit(solution)/shard_map/all_gather | solution.py:44
  27.8 138.7 %all-gather.11.cloned.1.call-start = ((), (), s32[]{:S(2)}) async-start(), calls=%async_computation.4 | async-start | bytes 1179648 | tf_op jit(solution)/shard_map/all_gather | solution.py:26
  57.3 161.1 %all-gather.7.cloned.1.call-start = ((), (), s32[]{:S(2)}) async-start(), calls=%async_computation.1 | async-start | bytes 9437184 | tf_op jit(solution)/shard_map/all_gather | solution.py:51
  231.9 24.1 %copy-start.1 = (s32[1,16]{1,0:T(1,128)S(1)}, s32[1,16]{1,0:T(1,128)}, u32[]{:S(2)}) copy-start(s32[1,16]{1,0:T(1,128)} %param.9) | copy-start | bytes 196
Sparse Core Ops, SparseCore 0:
  27.4 29.8 reduce-scatter.1
Sparse Core Ops, SparseCore 1:
  29.9 111.5 all-gather.8
  143.1 23.5 all-gather.10
  168.8 49.6 all-gather.6
where the time goes:
time: 312 us
  waiting for transfers between devices  130 us (42%)
  blocking collectives  78.7 us (25%)
  matrix products  43.4 us (14%)
  local copies, waits for them, and re-layouts  31.2 us (10%)
  between operations  19.8 us (6%)
  other arithmetic  8.28 us (3%)
    all_gather x1, waiting for transfers between devices, on_device(): lax.all_gather(band_tiles[:, :half], COL, axis=1, tiled=True)  51.8 us
    all_gather x1, waiting for transfers between devices, on_device(): lax.all_gather(matrix_tiles, ROW, axis=0, tiled=True)  35.1 us
    psum x4, blocking collectives, over_axes(): shard = lax.psum(shard, axis)  34.4 us
    reduce_scatter x1, waiting for transfers between devices, sum_by_parts(): lax.psum_scatter(rows_for(lines, lax.axis_size(axis)), axis, scatter_dime...  29.4 us
    dot_general x1, matrix products, on_device(): jnp.einsum('ap,axz->pxz', weights, product, precision=lax.Precision.HIGHEST)  24.1 us
    all_gather x1, blocking collectives, on_device(): lax.all_gather(matrix_live, ROW, axis=0, tiled=True)  17.3 us
    all_gather x1, blocking collectives, on_device(): lax.all_gather(matrix_col, ROW, axis=0, tiled=True)  17.2 us
    dot_general x1, matrix products, on_device(): jnp.einsum('axy,ayz->axz', tiles, picked, preferred_element_type=jnp.floa...  13.5 us
  transfers between devices with their start and end apart: 4, of which 4 were waited for; matrix products, arithmetic and copies ran while one was open for 8% of the time, Pallas kernels for 0%

commit v1 on v0

v1 whole, which is shorter than its diff:
```python
import functools

import jax
import jax.numpy as jnp
from jax import lax
from jax.experimental import pallas as pl
from jax.experimental.pallas import tpu as pltpu
from jax.sharding import PartitionSpec as P

TILE = 256
N_ROW, N_COL = 16, 8
SPOTS = 32
LOWER = 64
PRODUCTS = 72
ORDER = ((0, 0), (1, 0), (0, 1), (3, 0), (1, 1), (3, 1), (2, 0), (2, 1))
XA, XB, YA, YB = (0, 1), (0, 3), (1, 0), (3, 0)
MESH = pl.DeviceIdType.MESH


def tables(tab_v, enc_row, menc_row, y, x, col):
    shape = (128, 128)
    r = lax.broadcasted_iota(jnp.int32, shape, 0)
    l = lax.broadcasted_iota(jnp.int32, shape, 1)
    r1 = lax.broadcasted_iota(jnp.int32, (128, 1), 0)
    zero = jnp.zeros(shape, jnp.int32)
    eye = r == l

    def lanes(v):
        return jnp.sum(v, axis=1, keepdims=True)

    def to_row(column):
        return jnp.sum(jnp.where(eye, column + zero, 0), axis=0, keepdims=True)

    enc = enc_row + zero
    enc_col = lanes(jnp.where(eye, enc, 0))
    up_col = jnp.where(enc_col > 0, 1, 0) * ((r1 >> 3) & 1)
    rank_row = jnp.sum(jnp.where(r < l, up_col + zero, 0), axis=0, keepdims=True)
    up = jnp.where(enc > 0, 1, 0) * ((l >> 3) & 1)
    group = r1 >> 3
    source = jnp.zeros((128, 1), jnp.int32)
    for n, (dy, q) in enumerate(ORDER):
        source = jnp.where(group == n, ((y ^ dy) << 1) | ((x >> 1) ^ q), source)
    slot = (source << 4) + (r1 & 7)
    low_hit = jnp.where(l == slot + zero, 1, 0)
    up_hit = up * jnp.where(rank_row + zero == r - LOWER, 1, 0)
    pick = jnp.where(r < LOWER, low_hit, up_hit)
    cell_col = lanes(pick * enc)
    t_col = lanes(pick * l)
    cell = jnp.maximum(cell_col - 1, 0)
    kk, src = cell & 15, t_col >> 4
    menc_col = lanes(jnp.where(l == ((src << 4) + kk) + zero, menc_row + zero, 0))
    good = jnp.where(cell_col > 0, 1, 0) * jnp.where(menc_col > 0, 1, 0)
    pos_col = jnp.where(good > 0, ((cell >> 4) << 4) + menc_col - 1, -1)
    pos = pos_col + zero
    pos_row = to_row(pos_col)
    same = jnp.where(pos == pos_row + zero, 1, 0) * jnp.where(pos >= 0, 1, 0) * jnp.where(r < l, 1, 0)
    prev = jnp.max(jnp.where(same > 0, r, -1), axis=0, keepdims=True)
    last = jnp.max(jnp.where(pos == l, r, -1), axis=0, keepdims=True)
    own = jnp.where(enc_col + zero - 1 == l, 1, 0) * jnp.where((r >> 4) == col, 1, 0)
    base = jnp.max(jnp.where(own > 0, r & 15, -1), axis=0, keepdims=True)
    a_index = (((kk >> 3) ^ (x & 1)) << 3) | (kk & 7)
    tab_v[0:1, :] = to_row(a_index)
    tab_v[1:2, :] = jnp.where(prev < 0, PRODUCTS, prev)
    tab_v[2:3, :] = jnp.where(last < 0, PRODUCTS, last)
    tab_v[3:4, :] = jnp.where(base < 0, 16, base)
    tab_v[4:5, :] = to_row(((t_col >> 4) << 3) + (t_col & 7))
    tab_v[5:6, :] = to_row(src)
    tab_v[6:8, :] = jnp.zeros((2, 128), jnp.int32)


def kernel(
    cell_ref, count_ref, mcol_ref, mlive_ref, f_ref, a_ref, out_ref, gain_ref,
    a0, a1, a2, a3, a4, a5, a6, a7, fl, fu, fo, s_ref, picked, stage, mb, mm, tab_v, tab, gr, gc,
    a_send, a_recv, f_send, f_recv, m_send, m_recv, g_send, g_recv, local_sem, out_sem,
):
    row, col = lax.axis_index("row"), lax.axis_index("col")
    y, x, z, core = row >> 2, row & 3, col >> 1, col & 1
    groups = (a0, a1, a2, a3, a4, a5, a6, a7)

    barrier = pltpu.get_barrier_semaphore()
    for d in range(1, N_ROW):
        pl.semaphore_signal(barrier, inc=1, device_id=(row ^ d, col), device_id_type=MESH)
    for d in range(1, N_COL):
        pl.semaphore_signal(barrier, inc=1, device_id=(row, col ^ d), device_id_type=MESH)

    local = [
        pltpu.make_async_copy(a_ref, a0.at[pl.ds(0, 8)], local_sem.at[0]),
        pltpu.make_async_copy(f_ref.at[pl.ds(0, 8)], fl.at[pl.ds(col * 8, 8)], local_sem.at[1]),
        pltpu.make_async_copy(f_ref.at[pl.ds(8, 8)], fu.at[pl.ds(col * 8, 8)], local_sem.at[2]),
        pltpu.make_async_copy(f_ref, fo.at[pl.ds(0, 16)], local_sem.at[3]),
    ]
    for copy in local:
        copy.start()

    lane = lax.broadcasted_iota(jnp.int32, (8, 128), 1)
    own_b, own_m = jnp.zeros((8, 128), jnp.int32), jnp.zeros((8, 128), jnp.int32)
    for s in range(16):
        value = jnp.where(s < count_ref[0, 0], cell_ref[0, s] + 1, 0)
        own_b = jnp.where(lane == col * 16 + s, value, own_b)
    for s in range(8):
        value = jnp.where(mlive_ref[0, s] > 0, mcol_ref[0, s] + 1, 0)
        own_m = jnp.where(lane == row * 8 + s, value, own_m)
    mb[pl.ds(col, 1)] = own_b.reshape(1, 8, 128)
    mm[pl.ds(row, 1)] = own_m.reshape(1, 8, 128)

    pl.semaphore_wait(barrier, N_ROW + N_COL - 2)

    started = []

    def send(src, dst, send_sem, recv_sem, device):
        copy = pltpu.make_async_remote_copy(
            src_ref=src, dst_ref=dst, send_sem=send_sem, recv_sem=recv_sem,
            device_id=device, device_id_type=MESH,
        )
        copy.start()
        started.append(copy)

    def arrived(ref, sem):
        pltpu.make_async_remote_copy(
            src_ref=ref, dst_ref=ref, send_sem=m_send.at[0], recv_sem=sem,
            device_id=(row ^ 1, col), device_id_type=MESH,
        ).wait_recv()

    def a_block(dy, dx, q):
        return groups[dy * 2 + (dx >> 1)].at[pl.ds((dx & 1) * 8 + 2 * q, 2)]

    a_sent, a_here = [0], set()

    def a_wait(dy, dx, *quarters):
        for q in quarters:
            if (dy, dx) != (0, 0) and (dy, dx, q) not in a_here:
                a_here.add((dy, dx, q))
                arrived(a_block(dy, dx, q), a_recv.at[(dy * 4 + dx) * 4 + q])

    def a_send_to(link, dy, dx, *quarters):
        a_wait(dy, dx, *quarters)
        ly, lx = link
        to = ((y ^ ly) << 2) | (x ^ lx)
        for q in quarters:
            src = a_ref.at[pl.ds(2 * q, 2)] if (dy, dx) == (0, 0) else a_block(dy, dx, q)
            there = (dy ^ ly, dx ^ lx)
            send(
                src, a_block(*there, q), a_send.at[a_sent[0]],
                a_recv.at[(there[0] * 4 + there[1]) * 4 + q], (to, col),
            )
            a_sent[0] += 1

    def f_source(dz, dc):
        return ((z ^ dz) << 1) | (core ^ dc)

    def f_block(upper, source, h):
        return (fu if upper else fl).at[pl.ds(source * 8 + 4 * h, 4)]

    f_sent, f_here = [0], set()

    def f_wait(dz, dc, upper, h):
        if (dz, dc) != (0, 0) and (dz, dc, upper, h) not in f_here:
            f_here.add((dz, dc, upper, h))
            source = f_source(dz, dc)
            arrived(f_block(upper, source, h), f_recv.at[source * 4 + upper * 2 + h])

    def f_send_to(lz, lc, dz, upper, *halves):
        source = f_source(dz, 0)
        for h in halves:
            f_wait(dz, 0, upper, h)
            src = f_ref.at[pl.ds(8 * upper + 4 * h, 4)] if dz == 0 else f_block(upper, source, h)
            send(
                src, f_block(upper, source, h), f_send.at[f_sent[0]],
                f_recv.at[source * 4 + upper * 2 + h], (row, f_source(lz, lc)),
            )
            f_sent[0] += 1

    for d in range(1, N_COL):
        send(mb.at[pl.ds(col, 1)], mb.at[pl.ds(col, 1)], m_send.at[d], m_recv.at[col], (row, col ^ d))
    for d in range(1, N_ROW):
        send(mm.at[pl.ds(row, 1)], mm.at[pl.ds(row, 1)], m_send.at[8 + d], m_recv.at[8 + row], (row ^ d, col))
    for q in (0, 1):
        for link in (XA, XB):
            a_send_to(link, 0, 0, q)
        for link in (YA, YB):
            a_send_to(link, 0, 0, 2 + q)
        for lz in (1, 3):
            f_send_to(lz, 0, 0, 0, q)
    for q in (0, 1):
        for link in (XA, XB):
            a_send_to(link, 0, 0, 2 + q)
        for link in (YA, YB):
            a_send_to(link, 0, 0, q)
    f_send_to(0, 1, 0, 0, 0, 1)

    s_ref[PRODUCTS] = jnp.zeros((TILE, TILE), jnp.float32)
    fo[16] = jnp.zeros((TILE, TILE), jnp.bfloat16)
    for d in range(1, N_COL):
        arrived(mb.at[pl.ds(col ^ d, 1)], m_recv.at[col ^ d])
    for d in range(1, N_ROW):
        arrived(mm.at[pl.ds(row ^ d, 1)], m_recv.at[8 + (row ^ d)])
    enc_row = jnp.sum(mb[...], axis=0)[0:1, :]
    menc_row = jnp.sum(mm[...], axis=0)[0:1, :]
    tables(tab_v, enc_row, menc_row, y, x, col)
    to_scalars = pltpu.make_async_copy(tab_v, tab, local_sem.at[4])
    to_scalars.start()
    to_scalars.wait()

    def group_of(n):
        dy, q = ORDER[n]
        return groups[dy * 2 + q], ((y ^ dy) << 1) | ((x >> 1) ^ q)

    def products(n):
        a_group, source = group_of(n)
        for dx in (0, 1):
            a_wait(ORDER[n][0], 2 * ORDER[n][1] + dx, 0, 1, 2, 3)

        def lower(s, carry):
            o = n * 8 + s
            s_ref[o] = jnp.dot(
                fl[source * 8 + s], a_group[tab[0, o]], preferred_element_type=jnp.float32
            ) + s_ref[tab[1, o]]
            return carry

        lax.fori_loop(0, 8, lower, 0)

        def upper(j, carry):
            tile = a_group[tab[0, LOWER + j]]
            if n == 0:
                picked[j] = tile
            else:
                picked[j] = jnp.where(tab[5, LOWER + j] == source, tile, picked[j])
            return carry

        lax.fori_loop(0, 8, upper, 0)

    f_send_to(1, 0, 3, 0, 0)
    f_send_to(3, 0, 1, 0, 1)
    for h in (0, 1):
        for lz in (1, 3):
            f_send_to(lz, 0, 0, 1, h)
    a_send_to(XA, 0, 3, 0)
    a_send_to(XB, 0, 1, 1)
    a_send_to(YA, 3, 0, 2)
    a_send_to(YB, 1, 0, 3)
    for dx in (1, 3):
        for link in (YA, YB):
            a_send_to(link, 0, dx, 0, 1)
        for link in (XA, XB):
            a_send_to(link, dx, 0, 2, 3)
    f_send_to(0, 1, 1, 0, 0, 1)
    f_send_to(0, 1, 3, 0, 0, 1)
    f_send_to(0, 1, 0, 1, 0, 1)
    a_send_to(XA, 0, 3, 2)
    a_send_to(XB, 0, 1, 3)
    for link in (YA, YB):
        a_send_to(link, 0, 2, 0, 1)
    for link in (XA, XB):
        a_send_to(link, 2, 0, 2, 3)
    f_send_to(0, 1, 2, 0, 0, 1)
    f_send_to(1, 0, 3, 1, 0)
    f_send_to(3, 0, 1, 1, 1)
    a_send_to(YA, 3, 0, 0)
    a_send_to(YB, 1, 0, 1)
    a_send_to(XA, 1, 3, 2)
    a_send_to(XB, 1, 1, 3)
    for d in (1, 3):
        a_send_to(YA, 3, d, 0)
        a_send_to(YB, 1, d, 1)
    a_send_to(XA, 3, 3, 2)
    a_send_to(XB, 3, 1, 3)
    a_send_to(YA, 3, 2, 0)
    a_send_to(YB, 1, 2, 1)
    a_send_to(XA, 2, 3, 2)
    a_send_to(XB, 2, 1, 3)
    f_send_to(0, 1, 1, 1, 0, 1)
    f_send_to(0, 1, 3, 1, 0, 1)
    f_send_to(0, 1, 2, 1, 0, 1)

    for copy in local:
        copy.wait()
    for dz in range(4):
        for h in (0, 1):
            f_wait(dz, 1, 0, h)
    for n in range(8):
        products(n)
    for dz in range(4):
        for h in (0, 1):
            f_wait(dz, 1, 1, h)

    def spilled(j, carry):
        o = LOWER + j
        s_ref[o] = jnp.dot(
            fu[tab[4, o]], picked[j], preferred_element_type=jnp.float32
        ) + s_ref[tab[1, o]]
        return carry

    lax.fori_loop(0, 8, spilled, 0)

    outs = []
    total = jnp.zeros((8, TILE), jnp.float32)
    for i in range(2):

        def output(c, total):
            base = fo[tab[3, i * 16 + c]].astype(jnp.float32)
            full = jnp.minimum(1.0, base + s_ref[tab[2, i * 16 + c]])
            stage[pl.ds(i * TILE, TILE), pl.ds(pl.multiple_of(c * TILE, TILE), TILE)] = full.astype(jnp.bfloat16)
            return total + jnp.sum((full - base).reshape(TILE // 8, 8, TILE), axis=0)

        total = lax.fori_loop(0, 16, output, total)
        rows = pl.ds(i * TILE, TILE)
        copy = pltpu.make_async_copy(stage.at[rows], out_ref.at[rows], out_sem.at[i])
        copy.start()
        outs.append(copy)

    gr[pl.ds(row, 1)] = (total[:, :128] + total[:, 128:]).reshape(1, 8, 128)
    for d in range(1, N_ROW):
        send(gr.at[pl.ds(row, 1)], gr.at[pl.ds(row, 1)], g_send.at[d], g_recv.at[row], (row ^ d, col))
    for d in range(1, N_ROW):
        arrived(gr.at[pl.ds(row ^ d, 1)], g_recv.at[row ^ d])
    gc[pl.ds(col, 1)] = jnp.sum(gr[...], axis=0).reshape(1, 8, 128)
    for d in range(1, N_COL):
        send(gc.at[pl.ds(col, 1)], gc.at[pl.ds(col, 1)], g_send.at[16 + d], g_recv.at[16 + col], (row, col ^ d))
    for d in range(1, N_COL):
        arrived(gc.at[pl.ds(col ^ d, 1)], g_recv.at[16 + (col ^ d)])
    gain_ref[...] = jnp.sum(gc[...], axis=0)
    for copy in started:
        copy.wait_send()
    for copy in outs:
        copy.wait()


def on_device(band_tiles, band_cell, band_count, matrix_tiles, matrix_col, matrix_live):
    smem = pl.BlockSpec(memory_space=pltpu.SMEM)
    hbm = pl.BlockSpec(memory_space=pl.ANY)
    tiles = (TILE, TILE)
    reached, gain = pl.pallas_call(
        kernel,
        out_shape=(
            jax.ShapeDtypeStruct((2 * TILE, 16 * TILE), jnp.bfloat16),
            jax.ShapeDtypeStruct((8, 128), jnp.float32),
        ),
        in_specs=[smem] * 4 + [hbm] * 2,
        out_specs=(hbm, pl.BlockSpec(memory_space=pltpu.VMEM)),
        scratch_shapes=[pltpu.VMEM((16, *tiles), jnp.bfloat16)] * 8
        + [
            pltpu.VMEM((LOWER, *tiles), jnp.bfloat16),
            pltpu.VMEM((LOWER, *tiles), jnp.bfloat16),
            pltpu.VMEM((17, *tiles), jnp.bfloat16),
            pltpu.VMEM((PRODUCTS + 1, *tiles), jnp.float32),
            pltpu.VMEM((8, *tiles), jnp.bfloat16),
            pltpu.VMEM((2 * TILE, 16 * TILE), jnp.bfloat16),
            pltpu.VMEM((N_COL, 8, 128), jnp.int32),
            pltpu.VMEM((N_ROW, 8, 128), jnp.int32),
            pltpu.VMEM((8, 128), jnp.int32),
            pltpu.SMEM((8, 128), jnp.int32),
            pltpu.VMEM((N_ROW, 8, 128), jnp.float32),
            pltpu.VMEM((N_COL, 8, 128), jnp.float32),
            pltpu.SemaphoreType.DMA((60,)),
            pltpu.SemaphoreType.DMA((64,)),
            pltpu.SemaphoreType.DMA((28,)),
            pltpu.SemaphoreType.DMA((32,)),
            pltpu.SemaphoreType.DMA((24,)),
            pltpu.SemaphoreType.DMA((24,)),
            pltpu.SemaphoreType.DMA((24,)),
            pltpu.SemaphoreType.DMA((24,)),
            pltpu.SemaphoreType.DMA((5,)),
            pltpu.SemaphoreType.DMA((2,)),
        ],
        compiler_params=pltpu.CompilerParams(
            collective_id=0, has_side_effects=True, vmem_limit_bytes=60 * 1024 * 1024
        ),
    )(band_cell, band_count, matrix_col, matrix_live, band_tiles[0], matrix_tiles[0])
    return reached, jnp.sum(gain) / 268435456.0


def solution(mesh):
    placed = P("row", "col")
    tiled = P("row", "col", None, None)
    return jax.shard_map(
        on_device, mesh=mesh,
        in_specs=(tiled, placed, placed, tiled, placed, placed),
        out_specs=(placed, P()), check_vma=False,
    )
```

time: 312 us -> 124 us (0.40)
  waiting for transfers between devices: 130 us -> 0 us
  Pallas kernels: 0 us -> 114 us
  blocking collectives: 78.7 us -> 0 us
  matrix products: 43.4 us -> 0 us
  local copies, waits for them, and re-layouts: 31.2 us -> 4.7 us
  between operations: 19.8 us -> 3.07 us
  other arithmetic: 8.28 us -> 1.29 us
    pallas_call x0 -> x1, Pallas kernels: none -> 114 us  [on_device(): pl.pallas_call(kernel, out_shape=(jax.ShapeDtypeStruct((2 * TILE, 16 * TI...]
    all_gather x3 -> x0, waiting for transfers between devices: 100 us -> none  [the longest x1 51.8 us: on_device(): lax.all_gather(band_tiles[:, :half], COL, axis=1, tiled=True)]
    dot_general x4 -> x0, matrix products: 43.4 us -> none  [the longest x1 24.1 us: on_device(): jnp.einsum('ap,axz->pxz', weights, product, precision=lax.Precision.HIGHEST)]
    all_gather x2 -> x0, blocking collectives: 34.5 us -> none  [the longest x1 17.3 us: on_device(): lax.all_gather(matrix_live, ROW, axis=0, tiled=True)]
    psum x4 -> x0, blocking collectives: 34.4 us -> none  [over_axes(): shard = lax.psum(shard, axis)]
    reduce_scatter x1 -> x0, waiting for transfers between devices: 29.4 us -> none  [sum_by_parts(): lax.psum_scatter(rows_for(lines, lax.axis_size(axis)), axis, scatter_dime...]
    gather x7 -> x0, local copies, waits for them, and re-layouts: 17 us -> none  [the longest x1 11.8 us: on_device(): picked = jnp.take(flat_tiles, k_glob, axis=0)]
    unnamed x1 -> x0, blocking collectives: 9.78 us -> none
  transfers between devices with their start and end apart: 4 -> 0, of which waited for: 4 -> 0; matrix products, arithmetic and copies ran while one was open for 8% -> 0% of each run, Pallas kernels for 0% -> 0%
where the time goes in v1:
time: 124 us; the launch traced here: 123 us
  Pallas kernels  114 us (92%)
  local copies, waits for them, and re-layouts  4.7 us (4%)
  between operations  3.07 us (2%)
  other arithmetic  1.29 us (1%)
    pallas_call x1, Pallas kernels, on_device(): pl.pallas_call(kernel, out_shape=(jax.ShapeDtypeStruct((2 * TILE, 16 * TI...  114 us
    unnamed x1, local copies, waits for them, and re-layouts  4.7 us

profile of v1, /device:TPU:1, one launch (start us, length us, event | category | flops | bytes accessed | tf_op | source)
XLA Modules:
  0.0 123.4 jit_solution(15233503615089023915)
XLA Ops:
  1.3 114.4 %shard_map.77 = (bf16[512,4096]{1,0:T(8,128)(2,1)}, f32[8,128]{1,0:T(8,128)}) custom-call(s32[1,16]{1,0:T(1,128)} %cell_ref.1, s32[1,1]{1,0:T(1,128)S(6)} %copy.9.count_ref, s32[1,8]{1,0:T(1,128)} %mcol_ref.1, s32[1,8]{1,0:T(1,128)} %mlive_ref.1, bf16[16,256,256]{2,1,0:T(8,128)(2,1)} %bitcast.2, bf16[8,256,256]{2,1,0:T(8,128)(2,1)} %bitcast.3), custom_call_target="tpu_custom_call" | custom-call | tf_op jit(solution)/shard_map/pallas_call | solution.py:332
  115.6 1.3 %reduce_sum.9 = f32[]{:T(128)} reduce(f32[8,128]{1,0:T(8,128)} %get-tuple-element.5, f32[]{:T(128)} %constant.1.clone.1), dimensions={0,1}, to_apply=%region_0.0 | reduce | flops 1023 | bytes 4104 | tf_op jit(solution)/shard_map/reduce_sum | solution.py:369
  117.6 4.7 %copy.10 = bf16[512,4096]{1,0:T(8,128)(2,1)} copy(bf16[512,4096]{1,0:T(8,128)(2,1)} %get-tuple-element.8) | data formatting | bytes 8388608

commit v2 on v1

v2 whole, which is shorter than its diff:
```python
import functools

import jax
import jax.numpy as jnp
from jax import lax
from jax.experimental import pallas as pl
from jax.experimental.pallas import tpu as pltpu
from jax.sharding import PartitionSpec as P

TILE = 256
N_ROW, N_COL = 16, 8
SPOTS = 32
LOWER = 64
PRODUCTS = 72
ORDER = ((0, 0), (1, 0), (3, 0), (0, 1), (1, 1), (2, 0), (3, 1), (2, 1))
UNROLL = 4
DEPTH = 2
XA, XB, YA, YB = (0, 1), (0, 3), (1, 0), (3, 0)
NEAR_ROW, NEAR_COL = (1, 3, 4, 12), (2, 6, 1)
MESH = pl.DeviceIdType.MESH


def tables(tab_v, enc_row, menc_row, y, x, col):
    shape = (128, 128)
    r = lax.broadcasted_iota(jnp.int32, shape, 0)
    l = lax.broadcasted_iota(jnp.int32, shape, 1)
    r1 = lax.broadcasted_iota(jnp.int32, (128, 1), 0)
    zero = jnp.zeros(shape, jnp.int32)
    eye = r == l

    def lanes(v):
        return jnp.sum(v, axis=1, keepdims=True)

    def to_row(column):
        return jnp.sum(jnp.where(eye, column + zero, 0), axis=0, keepdims=True)

    enc = enc_row + zero
    enc_col = lanes(jnp.where(eye, enc, 0))
    up_col = jnp.where(enc_col > 0, 1, 0) * ((r1 >> 3) & 1)
    rank_row = jnp.sum(jnp.where(r < l, up_col + zero, 0), axis=0, keepdims=True)
    up = jnp.where(enc > 0, 1, 0) * ((l >> 3) & 1)
    group = r1 >> 3
    source = jnp.zeros((128, 1), jnp.int32)
    for n, (dy, q) in enumerate(ORDER):
        source = jnp.where(group == n, ((y ^ dy) << 1) | ((x >> 1) ^ q), source)
    slot = (source << 4) + (r1 & 7)
    low_hit = jnp.where(l == slot + zero, 1, 0)
    up_hit = up * jnp.where(rank_row + zero == r - LOWER, 1, 0)
    pick = jnp.where(r < LOWER, low_hit, up_hit)
    cell_col = lanes(pick * enc)
    t_col = lanes(pick * l)
    cell = jnp.maximum(cell_col - 1, 0)
    kk, src = cell & 15, t_col >> 4
    menc_col = lanes(jnp.where(l == ((src << 4) + kk) + zero, menc_row + zero, 0))
    good = jnp.where(cell_col > 0, 1, 0) * jnp.where(menc_col > 0, 1, 0)
    pos_col = jnp.where(good > 0, ((cell >> 4) << 4) + menc_col - 1, -1)
    pos = pos_col + zero
    pos_row = to_row(pos_col)
    same = jnp.where(pos == pos_row + zero, 1, 0) * jnp.where(pos >= 0, 1, 0) * jnp.where(r < l, 1, 0)
    prev = jnp.max(jnp.where(same > 0, r, -1), axis=0, keepdims=True)
    last = jnp.max(jnp.where(pos == l, r, -1), axis=0, keepdims=True)
    own = jnp.where(enc_col + zero - 1 == l, 1, 0) * jnp.where((r >> 4) == col, 1, 0)
    base = jnp.max(jnp.where(own > 0, r & 15, -1), axis=0, keepdims=True)
    a_index = (((kk >> 3) ^ (x & 1)) << 3) | (kk & 7)
    tab_v[0:1, :] = to_row(a_index)
    tab_v[1:2, :] = jnp.where(prev < 0, PRODUCTS, prev)
    tab_v[2:3, :] = jnp.where(last < 0, PRODUCTS, last)
    tab_v[3:4, :] = jnp.where(base < 0, 16, base)
    tab_v[4:5, :] = to_row(((t_col >> 4) << 3) + (t_col & 7))
    tab_v[5:6, :] = to_row(src)
    tab_v[6:8, :] = jnp.zeros((2, 128), jnp.int32)


def kernel(
    cell_in, count_in, mcol_in, mlive_in, f_ref, a_ref, out_ref, gain_ref,
    cell_ref, count_ref, mcol_ref, mlive_ref,
    a0, a1, a2, a3, a4, a5, a6, a7, fl, fu, fo, s_ref, picked, stage, mb, mm, mb_in, mm_in, tab_v, tab, gains,
    a_send, a_recv, f_send, f_recv, m_send, m_recv, g_send, g_recv, local_sem, out_sem,
):
    row, col = lax.axis_index("row"), lax.axis_index("col")
    y, x, z, core = row >> 2, row & 3, col >> 1, col & 1
    groups = (a0, a1, a2, a3, a4, a5, a6, a7)

    barrier = pltpu.get_barrier_semaphore()
    for d in NEAR_ROW:
        pl.semaphore_signal(barrier, inc=1, device_id=(row ^ d, col), device_id_type=MESH)
    for d in NEAR_COL:
        pl.semaphore_signal(barrier, inc=1, device_id=(row, col ^ d), device_id_type=MESH)

    scalars = [
        pltpu.make_async_copy(there, here, local_sem.at[5 + i])
        for i, (there, here) in enumerate(
            ((cell_in, cell_ref), (count_in, count_ref), (mcol_in, mcol_ref), (mlive_in, mlive_ref))
        )
    ]
    for copy in scalars:
        copy.start()
    local = [
        pltpu.make_async_copy(a_ref, a0.at[pl.ds(0, 8)], local_sem.at[0]),
        pltpu.make_async_copy(f_ref.at[pl.ds(0, 8)], fl.at[pl.ds(col * 8, 8)], local_sem.at[1]),
        pltpu.make_async_copy(f_ref.at[pl.ds(8, 8)], fu.at[pl.ds(col * 8, 8)], local_sem.at[2]),
        pltpu.make_async_copy(f_ref, fo.at[pl.ds(0, 16)], local_sem.at[3]),
    ]
    for copy in local:
        copy.start()

    pl.semaphore_wait(barrier, len(NEAR_ROW) + len(NEAR_COL))

    started = []

    def send(src, dst, send_sem, recv_sem, device, keep=True):
        copy = pltpu.make_async_remote_copy(
            src_ref=src, dst_ref=dst, send_sem=send_sem, recv_sem=recv_sem,
            device_id=device, device_id_type=MESH,
        )
        copy.start()
        if keep:
            started.append(copy)
        return copy

    def arrived(ref, sem):
        pltpu.make_async_remote_copy(
            src_ref=ref, dst_ref=ref, send_sem=m_send.at[0], recv_sem=sem,
            device_id=(row ^ 1, col), device_id_type=MESH,
        ).wait_recv()

    def a_block(dy, dx, q):
        return groups[dy * 2 + (dx >> 1)].at[pl.ds((dx & 1) * 8 + 2 * q, 2)]

    a_here, f_here = set(), set()

    def a_wait(dy, dx, *quarters):
        for q in quarters:
            if (dy, dx) != (0, 0) and (dy, dx, q) not in a_here:
                a_here.add((dy, dx, q))
                arrived(a_block(dy, dx, q), a_recv.at[(dy * 4 + dx) * 4 + q])

    def f_source(dz, dc):
        return ((z ^ dz) << 1) | (core ^ dc)

    def f_block(dz, dc, u, n=2):
        upper, first = u // 4, 2 * (u % 4)
        return (fu if upper else fl).at[pl.ds(f_source(dz, dc) * 8 + first, n)]

    def f_wait(dz, *units):
        for u in units:
            if dz and (dz, u) not in f_here:
                f_here.add((dz, u))
                arrived(f_block(dz, 0, u), f_recv.at[dz * 8 + u])

    def sib_wait(upper):
        for dz in range(4):
            for u in (4 * upper, 4 * upper + 2):
                arrived(f_block(dz, 1, u, 4), f_recv.at[32 + dz * 4 + u // 2])

    def sib_send(dz, *halves):
        for h in halves:
            f_wait(dz, 2 * h, 2 * h + 1)
            src = f_ref.at[pl.ds(4 * h, 4)] if dz == 0 else f_block(dz, 0, 2 * h, 4)
            send(
                src, f_block(dz, 0, 2 * h, 4), f_send.at[24 + dz * 4 + h],
                f_recv.at[32 + dz * 4 + h], (row, col ^ 1),
            )

    def x_link(near, part):
        turn = [((0, 0), 0), ((0, 0), 1), ((0, 0), 2), ((0, near), part), ((0, 0), 3)]
        turn += [((dy, 0), q) for dy in (1, 3, 2) for q in (2, 3)]
        return turn + [((dy, near), part + 2) for dy in (0, 1, 3, 2)]

    def y_link(near, part):
        turn = [((0, 0), 2), ((0, 0), 3), ((0, 0), 0), ((near, 0), part + 2), ((0, 0), 1)]
        turn += [((0, dx), q) for dx in (1, 3, 2) for q in (0, 1)]
        return turn + [((near, dx), part) for dx in (0, 1, 3, 2)]

    def z_link(near, part):
        turn = [(0, u) for u in range(4)] + [(near, 2 * part), (near, 2 * part + 1)]
        return turn + [(0, u) for u in range(4, 8)] + [(near, 4 + 2 * part), (near, 5 + 2 * part)]

    a_links = ((XA, x_link(3, 0)), (YA, y_link(3, 0)), (XB, x_link(1, 1)), (YB, y_link(1, 1)))
    z_links = ((1, z_link(3, 0)), (3, z_link(1, 1)))
    flying = {}

    def pace(link):
        queue = flying.setdefault(link, [])
        if len(queue) == DEPTH:
            queue.pop(0).wait_send()
        return queue

    def turn(k):
        for i, ((ly, lx), order) in enumerate(a_links):
            (dy, dx), q = order[k]
            queue = pace(i)
            a_wait(dy, dx, q)
            src = a_ref.at[pl.ds(2 * q, 2)] if (dy, dx) == (0, 0) else a_block(dy, dx, q)
            there = (dy ^ ly, dx ^ lx)
            queue.append(send(
                src, a_block(*there, q), a_send.at[i * 15 + k],
                a_recv.at[(there[0] * 4 + there[1]) * 4 + q],
                (((y ^ ly) << 2) | (x ^ lx), col), False,
            ))
        if k < 12:
            for i, (lz, order) in enumerate(z_links):
                dz, u = order[k]
                queue = pace(4 + i)
                f_wait(dz, u)
                src = f_ref.at[pl.ds(2 * u, 2)] if dz == 0 else f_block(dz, 0, u)
                queue.append(send(
                    src, f_block(dz, 0, u), f_send.at[i * 12 + k],
                    f_recv.at[(dz ^ lz) * 8 + u], (row, f_source(lz, 0)), False,
                ))

    def own_rows():
        for copy in scalars:
            copy.wait()
        lane = lax.broadcasted_iota(jnp.int32, (8, 128), 1)
        own_b, own_m = jnp.zeros((8, 128), jnp.int32), jnp.zeros((8, 128), jnp.int32)
        for s in range(16):
            value = jnp.where(s < count_ref[0, 0], cell_ref[0, s] + 1, 0)
            own_b = jnp.where(lane == col * 16 + s, value, own_b)
        for s in range(8):
            value = jnp.where(mlive_ref[0, s] > 0, mcol_ref[0, s] + 1, 0)
            own_m = jnp.where(lane == row * 8 + s, value, own_m)
        mb[0] = own_b
        mm[0] = own_m

    def m_exchange(k):
        if k < 4:
            send(mm.at[k], mm_in.at[k], m_send.at[k], m_recv.at[k], (row ^ NEAR_ROW[k], col))
        if k < 3:
            send(mb.at[k], mb_in.at[k], m_send.at[4 + k], m_recv.at[4 + k], (row, col ^ NEAR_COL[k]))

    def m_add(k):
        if k < 4:
            arrived(mm_in.at[k], m_recv.at[k])
            mm[k + 1] = mm[k] + mm_in[k]
        if k < 3:
            arrived(mb_in.at[k], m_recv.at[4 + k])
            mb[k + 1] = mb[k] + mb_in[k]

    s_ref[PRODUCTS] = jnp.zeros((TILE, TILE), jnp.float32)
    fo[16] = jnp.zeros((TILE, TILE), jnp.bfloat16)

    def group_of(n):
        dy, q = ORDER[n]
        return groups[dy * 2 + q], ((y ^ dy) << 1) | ((x >> 1) ^ q)

    def products(n):
        a_group, source = group_of(n)
        for dx in (0, 1):
            a_wait(ORDER[n][0], 2 * ORDER[n][1] + dx, 0, 1, 2, 3)

        def lower(s, carry):
            o = n * 8 + s
            s_ref[o] = jnp.dot(
                fl[source * 8 + s], a_group[tab[0, o]], preferred_element_type=jnp.float32
            ) + s_ref[tab[1, o]]
            return carry

        lax.fori_loop(0, 8, lower, 0, unroll=UNROLL)

        def upper(j, carry):
            tile = a_group[tab[0, LOWER + j]]
            if n == 0:
                picked[j] = tile
            else:
                picked[j] = jnp.where(tab[5, LOWER + j] == source, tile, picked[j])
            return carry

        lax.fori_loop(0, 8, upper, 0)

    for k in range(15):
        turn(k)
        if k == 0:
            own_rows()
            m_exchange(0)
        if k in (1, 3, 5):
            m_add(k // 2)
            m_exchange(k // 2 + 1)
        if k == 2:
            sib_send(0, 0, 1, 2, 3)
        if k == 6:
            sib_send(1, 0, 1)
            sib_send(3, 0, 1)
        if k == 7:
            m_add(3)
            tables(tab_v, mb[3, 0:1, :], mm[4, 0:1, :], y, x, col)
            to_scalars = pltpu.make_async_copy(tab_v, tab, local_sem.at[4])
            to_scalars.start()
            to_scalars.wait()
        if k == 8:
            sib_send(2, 0, 1)
        if k == 10:
            for copy in local:
                copy.wait()
            sib_wait(0)
            products(0)
        if k == 11:
            products(1)
            products(2)
        if k == 12:
            sib_send(1, 2, 3)
            sib_send(3, 2, 3)
        if k == 13:
            products(3)
    sib_send(2, 2, 3)
    for n in range(4, 8):
        products(n)
    sib_wait(1)

    def spilled(j, carry):
        o = LOWER + j
        s_ref[o] = jnp.dot(
            fu[tab[4, o]], picked[j], preferred_element_type=jnp.float32
        ) + s_ref[tab[1, o]]
        return carry

    lax.fori_loop(0, 8, spilled, 0, unroll=UNROLL)

    outs = []
    total = jnp.zeros((8, TILE), jnp.float32)
    for i in range(2):

        def output(c, total):
            base = fo[tab[3, i * 16 + c]].astype(jnp.float32)
            full = jnp.minimum(1.0, base + s_ref[tab[2, i * 16 + c]])
            stage[pl.ds(i * TILE, TILE), pl.ds(pl.multiple_of(c * TILE, TILE), TILE)] = full.astype(jnp.bfloat16)
            return total + jnp.sum((full - base).reshape(TILE // 8, 8, TILE), axis=0)

        total = lax.fori_loop(0, 16, output, total, unroll=2)
        rows = pl.ds(i * TILE, TILE)
        copy = pltpu.make_async_copy(stage.at[rows], out_ref.at[rows], out_sem.at[i])
        copy.start()
        outs.append(copy)

    part = total[:, :128] + total[:, 128:]
    for k, n in enumerate((N_ROW, N_COL)):
        gains[k, 0] = part
        for d in range(1, n):
            device = (row, col ^ d) if k else (row ^ d, col)
            send(gains.at[k, 0], gains.at[k, d], g_send.at[k * N_ROW + d], g_recv.at[k], device)
        arrived(gains.at[k, pl.ds(1, n - 1)], g_recv.at[k])
        parts = [gains[k, d] for d in range(n)]
        while len(parts) > 1:
            parts = [parts[2 * i] + parts[2 * i + 1] for i in range(len(parts) // 2)]
        part = parts[0]
    gain_ref[0, 0] = jnp.sum(part) * (1.0 / 268435456.0)
    for queue in flying.values():
        started.extend(queue)
    for copy in started:
        copy.wait_send()
    for copy in outs:
        copy.wait()


def store_kernel(from_ref, to_ref, held, sem_in, sem_out):
    rows = [pl.ds(64 * i, 64) for i in range(8)]
    ins = [pltpu.make_async_copy(from_ref.at[r], held.at[r], sem_in.at[i]) for i, r in enumerate(rows)]
    outs = [pltpu.make_async_copy(held.at[r], to_ref.at[r], sem_out.at[i]) for i, r in enumerate(rows)]
    for copy in ins:
        copy.start()
    for into, out in zip(ins, outs):
        into.wait()
        out.start()
    for copy in outs:
        copy.wait()


def on_device(band_tiles, band_cell, band_count, matrix_tiles, matrix_col, matrix_live):
    smem = pl.BlockSpec(memory_space=pltpu.SMEM)
    hbm = pl.BlockSpec(memory_space=pl.ANY)
    tiles = (TILE, TILE)
    reached, gain = pl.pallas_call(
        kernel,
        out_shape=(
            jax.ShapeDtypeStruct((2 * TILE, 16 * TILE), jnp.bfloat16),
            jax.ShapeDtypeStruct((1, 1), jnp.float32),
        ),
        in_specs=[hbm] * 6,
        out_specs=(hbm, smem),
        scratch_shapes=[pltpu.SMEM((1, n), jnp.int32) for n in (16, 1, 8, 8)]
        + [pltpu.VMEM((16, *tiles), jnp.bfloat16)] * 8
        + [
            pltpu.VMEM((LOWER, *tiles), jnp.bfloat16),
            pltpu.VMEM((LOWER, *tiles), jnp.bfloat16),
            pltpu.VMEM((17, *tiles), jnp.bfloat16),
            pltpu.VMEM((PRODUCTS + 1, *tiles), jnp.float32),
            pltpu.VMEM((8, *tiles), jnp.bfloat16),
            pltpu.VMEM((2 * TILE, 16 * TILE), jnp.bfloat16),
            pltpu.VMEM((4, 8, 128), jnp.int32),
            pltpu.VMEM((5, 8, 128), jnp.int32),
            pltpu.VMEM((3, 8, 128), jnp.int32),
            pltpu.VMEM((4, 8, 128), jnp.int32),
            pltpu.VMEM((8, 128), jnp.int32),
            pltpu.SMEM((8, 128), jnp.int32),
            pltpu.VMEM((2, N_ROW, 8, 128), jnp.float32),
            pltpu.SemaphoreType.DMA((60,)),
            pltpu.SemaphoreType.DMA((64,)),
            pltpu.SemaphoreType.DMA((40,)),
            pltpu.SemaphoreType.DMA((48,)),
            pltpu.SemaphoreType.DMA((7,)),
            pltpu.SemaphoreType.DMA((7,)),
            pltpu.SemaphoreType.DMA((24,)),
            pltpu.SemaphoreType.DMA((2,)),
            pltpu.SemaphoreType.DMA((9,)),
            pltpu.SemaphoreType.DMA((2,)),
        ],
        compiler_params=pltpu.CompilerParams(
            collective_id=0, has_side_effects=True, vmem_limit_bytes=60 * 1024 * 1024
        ),
    )(band_cell, band_count, matrix_col, matrix_live, band_tiles[0], matrix_tiles[0])
    reached = pl.pallas_call(
        store_kernel,
        out_shape=jax.ShapeDtypeStruct((2 * TILE, 16 * TILE), jnp.bfloat16),
        in_specs=[hbm],
        out_specs=hbm,
        scratch_shapes=[
            pltpu.VMEM((2 * TILE, 16 * TILE), jnp.bfloat16),
            pltpu.SemaphoreType.DMA((8,)),
            pltpu.SemaphoreType.DMA((8,)),
        ],
        compiler_params=pltpu.CompilerParams(vmem_limit_bytes=60 * 1024 * 1024),
    )(reached)
    return reached, gain.reshape(())


def solution(mesh):
    placed = P("row", "col")
    tiled = P("row", "col", None, None)
    return jax.shard_map(
        on_device, mesh=mesh,
        in_specs=(tiled, placed, placed, tiled, placed, placed),
        out_specs=(placed, P()), check_vma=False,
    )
```

time: 124 us -> 116 us (0.935)
  local copies, waits for them, and re-layouts: 4.7 us -> 0 us
  other arithmetic: 1.29 us -> 0 us
    pallas_call x1, Pallas kernels: 114 us -> 109 us  [on_device(): pl.pallas_call(kernel, out_shape=(jax.ShapeDtypeStruct((2 * TILE, 16 * TI...]
    unnamed x1 -> x0, local copies, waits for them, and re-layouts: 4.7 us -> none
    pallas_call x0 -> x1, Pallas kernels: none -> 3.58 us  [on_device(): pl.pallas_call(store_kernel, out_shape=jax.ShapeDtypeStruct((2 * TILE, 16...]
    reduce_sum x1 -> x0, other arithmetic: 1.29 us -> none  [on_device(): return (reached, jnp.sum(gain) / 268435456.0)]
where the time goes in v2:
time: 116 us
  Pallas kernels  113 us (97%)
  between operations  3.02 us (3%)
    pallas_call x1, Pallas kernels, on_device(): pl.pallas_call(kernel, out_shape=(jax.ShapeDtypeStruct((2 * TILE, 16 * TI...  109 us
    pallas_call x1, Pallas kernels, on_device(): pl.pallas_call(store_kernel, out_shape=jax.ShapeDtypeStruct((2 * TILE, 16...  3.58 us

profile of v2, /device:TPU:1, one launch (start us, length us, event | category | flops | bytes accessed | tf_op | source)
XLA Modules:
  0.0 116.0 jit_solution(13289847858687045151)
XLA Ops:
  1.3 109.4 %shard_map.77 = (bf16[512,4096]{1,0:T(8,128)(2,1)}, f32[1,1]{1,0:T(1,128)}) custom-call(s32[1,16]{1,0:T(1,128)} %cell_in.1, s32[1,1]{1,0:T(1,128)S(6)} %copy.9.count_in, s32[1,8]{1,0:T(1,128)} %mcol_in.1, s32[1,8]{1,0:T(1,128)} %mlive_in.1, bf16[16,256,256]{2,1,0:T(8,128)(2,1)} %bitcast.3, bf16[8,256,256]{2,1,0:T(8,128)(2,1)} %bitcast.4), custom_call_target="tpu_custom_call" | custom-call | tf_op jit(solution)/shard_map/pallas_call | solution.py:372
  110.6 3.6 %shard_map.78 = bf16[512,4096]{1,0:T(8,128)(2,1)} custom-call(bf16[512,4096]{1,0:T(8,128)(2,1)} %get-tuple-element.4.from_ref), custom_call_target="tpu_custom_call" | custom-call | tf_op jit(solution)/shard_map/pallas_call | solution.py:411

commit v3 on v2

--- a/solution.py
+++ b/solution.py
@@ -12,11 +12,13 @@
 SPOTS = 32
 LOWER = 64
 PRODUCTS = 72
+BLANK = PRODUCTS + 16
 ORDER = ((0, 0), (1, 0), (3, 0), (0, 1), (1, 1), (2, 0), (3, 1), (2, 1))
-UNROLL = 4
+UNROLL = 8
 DEPTH = 2
 XA, XB, YA, YB = (0, 1), (0, 3), (1, 0), (3, 0)
 NEAR_ROW, NEAR_COL = (1, 3, 4, 12), (2, 6, 1)
+FAR_FIRST = (10, 9, 11, 6, 14, 2, 8, 5, 7, 13, 15, 1, 3, 4, 12)
 MESH = pl.DeviceIdType.MESH
 
 
@@ -59,23 +61,27 @@
     same = jnp.where(pos == pos_row + zero, 1, 0) * jnp.where(pos >= 0, 1, 0) * jnp.where(r < l, 1, 0)
     prev = jnp.max(jnp.where(same > 0, r, -1), axis=0, keepdims=True)
     last = jnp.max(jnp.where(pos == l, r, -1), axis=0, keepdims=True)
-    own = jnp.where(enc_col + zero - 1 == l, 1, 0) * jnp.where((r >> 4) == col, 1, 0)
-    base = jnp.max(jnp.where(own > 0, r & 15, -1), axis=0, keepdims=True)
+    own = jnp.where((r1 >> 4) == col, 1, 0)
+    own_at = own * jnp.where(enc_col > 0, 1, 0)
+    base = jnp.max(jnp.where((own_at * enc_col + zero) == l + 1, r & 15, -1), axis=0, keepdims=True)
+    base = jnp.where(base < 0, BLANK, PRODUCTS + base)
+    base_col = lanes(jnp.where(pos == l, base + zero, 0))
+    base_of = to_row(jnp.where(pos_col < 0, BLANK, base_col))
     a_index = (((kk >> 3) ^ (x & 1)) << 3) | (kk & 7)
     tab_v[0:1, :] = to_row(a_index)
-    tab_v[1:2, :] = jnp.where(prev < 0, PRODUCTS, prev)
-    tab_v[2:3, :] = jnp.where(last < 0, PRODUCTS, last)
-    tab_v[3:4, :] = jnp.where(base < 0, 16, base)
+    tab_v[1:2, :] = jnp.where(prev < 0, base_of, prev)
+    tab_v[2:3, :] = jnp.where(last < 0, base, last)
+    tab_v[3:4, :] = to_row(good)
     tab_v[4:5, :] = to_row(((t_col >> 4) << 3) + (t_col & 7))
     tab_v[5:6, :] = to_row(src)
     tab_v[6:8, :] = jnp.zeros((2, 128), jnp.int32)
 
 
 def kernel(
-    cell_in, count_in, mcol_in, mlive_in, f_ref, a_ref, out_ref, gain_ref,
+    cell_in, count_in, mcol_in, mlive_in, f_ref, a_ref, out_ref,
     cell_ref, count_ref, mcol_ref, mlive_ref,
-    a0, a1, a2, a3, a4, a5, a6, a7, fl, fu, fo, s_ref, picked, stage, mb, mm, mb_in, mm_in, tab_v, tab, gains,
-    a_send, a_recv, f_send, f_recv, m_send, m_recv, g_send, g_recv, local_sem, out_sem,
+    a0, a1, a2, a3, a4, a5, a6, a7, fl, fu, s_ref, picked, mb, mm, mb_in, mm_in, tab_v, tab, gains,
+    a_send, a_recv, f_send, f_recv, m_send, m_recv, g_send, g_recv, local_sem,
 ):
     row, col = lax.axis_index("row"), lax.axis_index("col")
     y, x, z, core = row >> 2, row & 3, col >> 1, col & 1
@@ -99,7 +105,6 @@
         pltpu.make_async_copy(a_ref, a0.at[pl.ds(0, 8)], local_sem.at[0]),
         pltpu.make_async_copy(f_ref.at[pl.ds(0, 8)], fl.at[pl.ds(col * 8, 8)], local_sem.at[1]),
         pltpu.make_async_copy(f_ref.at[pl.ds(8, 8)], fu.at[pl.ds(col * 8, 8)], local_sem.at[2]),
-        pltpu.make_async_copy(f_ref, fo.at[pl.ds(0, 16)], local_sem.at[3]),
     ]
     for copy in local:
         copy.start()
@@ -237,26 +242,29 @@
             arrived(mb_in.at[k], m_recv.at[4 + k])
             mb[k + 1] = mb[k] + mb_in[k]
 
-    s_ref[PRODUCTS] = jnp.zeros((TILE, TILE), jnp.float32)
-    fo[16] = jnp.zeros((TILE, TILE), jnp.bfloat16)
+    s_ref[BLANK] = jnp.zeros((TILE, TILE), jnp.float32)
 
     def group_of(n):
         dy, q = ORDER[n]
         return groups[dy * 2 + q], ((y ^ dy) << 1) | ((x >> 1) ^ q)
 
-    def products(n):
+    def add_product(o, f_tile, a_tile, gain):
+        before = s_ref[tab[1, o]]
+        after = jnp.dot(f_tile, a_tile, preferred_element_type=jnp.float32) + before
+        s_ref[o] = after
+        more = (jnp.minimum(1.0, after) - jnp.minimum(1.0, before)).reshape(8, TILE // 8, TILE)
+        return gain + jnp.where(tab[3, o] > 0, jnp.sum(more, axis=0), 0.0)
+
+    def products(n, gain):
         a_group, source = group_of(n)
         for dx in (0, 1):
             a_wait(ORDER[n][0], 2 * ORDER[n][1] + dx, 0, 1, 2, 3)
 
-        def lower(s, carry):
+        def lower(s, gain):
             o = n * 8 + s
-            s_ref[o] = jnp.dot(
-                fl[source * 8 + s], a_group[tab[0, o]], preferred_element_type=jnp.float32
-            ) + s_ref[tab[1, o]]
-            return carry
-
-        lax.fori_loop(0, 8, lower, 0, unroll=UNROLL)
+            return add_product(o, fl[source * 8 + s], a_group[tab[0, o]], gain)
+
+        gain = lax.fori_loop(0, 8, lower, gain, unroll=UNROLL)
 
         def upper(j, carry):
             tile = a_group[tab[0, LOWER + j]]
@@ -267,7 +275,9 @@
             return carry
 
         lax.fori_loop(0, 8, upper, 0)
-
+        return gain
+
+    total = jnp.zeros((TILE // 8, TILE), jnp.float32)
     for k in range(15):
         turn(k)
         if k == 0:
@@ -293,99 +303,96 @@
             for copy in local:
                 copy.wait()
             sib_wait(0)
-            products(0)
+
+            def widen(s, carry):
+                s_ref[PRODUCTS + s] = fl[col * 8 + s].astype(jnp.float32)
+                s_ref[PRODUCTS + 8 + s] = fu[col * 8 + s].astype(jnp.float32)
+                return carry
+
+            lax.fori_loop(0, 8, widen, 0)
+            total = products(0, total)
         if k == 11:
-            products(1)
-            products(2)
+            total = products(1, total)
+            total = products(2, total)
         if k == 12:
             sib_send(1, 2, 3)
             sib_send(3, 2, 3)
         if k == 13:
-            products(3)
+            total = products(3, total)
     sib_send(2, 2, 3)
     for n in range(4, 8):
-        products(n)
+        total = products(n, total)
     sib_wait(1)
 
-    def spilled(j, carry):
+    def spilled(j, gain):
         o = LOWER + j
-        s_ref[o] = jnp.dot(
-            fu[tab[4, o]], picked[j], preferred_element_type=jnp.float32
-        ) + s_ref[tab[1, o]]
+        return add_product(o, fu[tab[4, o]], picked[j], gain)
+
+    total = lax.fori_loop(0, 8, spilled, total, unroll=UNROLL)
+
+    def output(c, carry):
+        for i in range(2):
+            out_ref[pl.ds(i * TILE, TILE), pl.ds(pl.multiple_of(c * TILE, TILE), TILE)] = jnp.minimum(
+                1.0, s_ref[tab[2, i * 16 + c]]
+            ).astype(jnp.bfloat16)
         return carry
 
-    lax.fori_loop(0, 8, spilled, 0, unroll=UNROLL)
-
-    outs = []
-    total = jnp.zeros((8, TILE), jnp.float32)
-    for i in range(2):
-
-        def output(c, total):
-            base = fo[tab[3, i * 16 + c]].astype(jnp.float32)
-            full = jnp.minimum(1.0, base + s_ref[tab[2, i * 16 + c]])
-            stage[pl.ds(i * TILE, TILE), pl.ds(pl.multiple_of(c * TILE, TILE), TILE)] = full.astype(jnp.bfloat16)
-            return total + jnp.sum((full - base).reshape(TILE // 8, 8, TILE), axis=0)
-
-        total = lax.fori_loop(0, 16, output, total, unroll=2)
-        rows = pl.ds(i * TILE, TILE)
-        copy = pltpu.make_async_copy(stage.at[rows], out_ref.at[rows], out_sem.at[i])
-        copy.start()
-        outs.append(copy)
-
+    total = jnp.sum(total.reshape(TILE // 64, 8, TILE), axis=0)
     part = total[:, :128] + total[:, 128:]
     for k, n in enumerate((N_ROW, N_COL)):
         gains[k, 0] = part
-        for d in range(1, n):
+        for d in FAR_FIRST if k == 0 else range(n - 1, 0, -1):
             device = (row, col ^ d) if k else (row ^ d, col)
             send(gains.at[k, 0], gains.at[k, d], g_send.at[k * N_ROW + d], g_recv.at[k], device)
+        if k == 0:
+            lax.fori_loop(0, 16, output, 0)
         arrived(gains.at[k, pl.ds(1, n - 1)], g_recv.at[k])
         parts = [gains[k, d] for d in range(n)]
         while len(parts) > 1:
             parts = [parts[2 * i] + parts[2 * i + 1] for i in range(len(parts) // 2)]
         part = parts[0]
-    gain_ref[0, 0] = jnp.sum(part) * (1.0 / 268435456.0)
+    rest = jnp.zeros((16, 128), jnp.float32) + jnp.sum(part) * (1.0 / 268435456.0)
+    for k in range(3):
+        piece = rest.astype(jnp.bfloat16)
+        out_ref[pl.ds(2 * TILE, 16), pl.ds(k * 128, 128)] = piece
+        rest = rest - piece.astype(jnp.float32)
     for queue in flying.values():
         started.extend(queue)
     for copy in started:
         copy.wait_send()
-    for copy in outs:
+
+
+def store_kernel(from_ref, to_ref, gain_ref, gain_s, sem):
+    rows = [pl.ds(128 * i, 128) for i in range(4)]
+    copies = [pltpu.make_async_copy(from_ref.at[r], to_ref.at[r], sem.at[i]) for i, r in enumerate(rows)]
+    for copy in copies:
+        copy.start()
+    gain = jnp.zeros((16, 128), jnp.float32)
+    for k in (2, 1, 0):
+        gain += from_ref[pl.ds(2 * TILE, 16), pl.ds(k * 128, 128)].astype(jnp.float32)
+    gain_s[0, 0] = gain[0, 0]
+    copies.append(pltpu.make_async_copy(gain_s, gain_ref, sem.at[4]))
+    copies[-1].start()
+    for copy in copies:
         copy.wait()
 
 
-def store_kernel(from_ref, to_ref, held, sem_in, sem_out):
-    rows = [pl.ds(64 * i, 64) for i in range(8)]
-    ins = [pltpu.make_async_copy(from_ref.at[r], held.at[r], sem_in.at[i]) for i, r in enumerate(rows)]
-    outs = [pltpu.make_async_copy(held.at[r], to_ref.at[r], sem_out.at[i]) for i, r in enumerate(rows)]
-    for copy in ins:
-        copy.start()
-    for into, out in zip(ins, outs):
-        into.wait()
-        out.start()
-    for copy in outs:
-        copy.wait()
-
-
 def on_device(band_tiles, band_cell, band_count, matrix_tiles, matrix_col, matrix_live):
-    smem = pl.BlockSpec(memory_space=pltpu.SMEM)
+    vmem = pl.BlockSpec(memory_space=pltpu.VMEM)
     hbm = pl.BlockSpec(memory_space=pl.ANY)
     tiles = (TILE, TILE)
-    reached, gain = pl.pallas_call(
+    both = pl.pallas_call(
         kernel,
-        out_shape=(
-            jax.ShapeDtypeStruct((2 * TILE, 16 * TILE), jnp.bfloat16),
-            jax.ShapeDtypeStruct((1, 1), jnp.float32),
-        ),
+        out_shape=pltpu.VMEM((2 * TILE + 16, 16 * TILE), jnp.bfloat16),
         in_specs=[hbm] * 6,
-        out_specs=(hbm, smem),
+        out_specs=vmem,
         scratch_shapes=[pltpu.SMEM((1, n), jnp.int32) for n in (16, 1, 8, 8)]
         + [pltpu.VMEM((16, *tiles), jnp.bfloat16)] * 8
         + [
             pltpu.VMEM((LOWER, *tiles), jnp.bfloat16),
             pltpu.VMEM((LOWER, *tiles), jnp.bfloat16),
-            pltpu.VMEM((17, *tiles), jnp.bfloat16),
-            pltpu.VMEM((PRODUCTS + 1, *tiles), jnp.float32),
+            pltpu.VMEM((BLANK + 1, *tiles), jnp.float32),
             pltpu.VMEM((8, *tiles), jnp.bfloat16),
-            pltpu.VMEM((2 * TILE, 16 * TILE), jnp.bfloat16),
             pltpu.VMEM((4, 8, 128), jnp.int32),
             pltpu.VMEM((5, 8, 128), jnp.int32),
             pltpu.VMEM((3, 8, 128), jnp.int32),
@@ -402,24 +409,22 @@
             pltpu.SemaphoreType.DMA((24,)),
             pltpu.SemaphoreType.DMA((2,)),
             pltpu.SemaphoreType.DMA((9,)),
-            pltpu.SemaphoreType.DMA((2,)),
         ],
         compiler_params=pltpu.CompilerParams(
-            collective_id=0, has_side_effects=True, vmem_limit_bytes=60 * 1024 * 1024
+            collective_id=0, has_side_effects=True, vmem_limit_bytes=57 * 1024 * 1024
         ),
     )(band_cell, band_count, matrix_col, matrix_live, band_tiles[0], matrix_tiles[0])
-    reached = pl.pallas_call(
+    reached, gain = pl.pallas_call(
         store_kernel,
-        out_shape=jax.ShapeDtypeStruct((2 * TILE, 16 * TILE), jnp.bfloat16),
-        in_specs=[hbm],
-        out_specs=hbm,
-        scratch_shapes=[
-            pltpu.VMEM((2 * TILE, 16 * TILE), jnp.bfloat16),
-            pltpu.SemaphoreType.DMA((8,)),
-            pltpu.SemaphoreType.DMA((8,)),
-        ],
-        compiler_params=pltpu.CompilerParams(vmem_limit_bytes=60 * 1024 * 1024),
-    )(reached)
+        out_shape=(
+            jax.ShapeDtypeStruct((2 * TILE, 16 * TILE), jnp.bfloat16),
+            jax.ShapeDtypeStruct((1, 1), jnp.float32),
+        ),
+        in_specs=[vmem],
+        out_specs=(hbm, hbm),
+        scratch_shapes=[pltpu.SMEM((1, 1), jnp.float32), pltpu.SemaphoreType.DMA((5,))],
+        compiler_params=pltpu.CompilerParams(vmem_limit_bytes=1024 * 1024),
+    )(pltpu.with_memory_space_constraint(both, pltpu.VMEM))
     return reached, gain.reshape(())
 
 

time: 116 us -> 110 us (0.948)
  Pallas kernels: 113 us -> 108 us
  between operations: 3.02 us -> 1.28 us
    pallas_call x2, Pallas kernels: 113 us -> 108 us  [the longest x1 106 us: on_device(): pl.pallas_call(kernel, out_shape=pltpu.VMEM((2 * TILE + 16, 16 * TILE), j...]
where the time goes in v3:
time: 110 us
  Pallas kernels  108 us (98%)
  between operations  1.28 us (1%)
    pallas_call x1, Pallas kernels, on_device(): pl.pallas_call(kernel, out_shape=pltpu.VMEM((2 * TILE + 16, 16 * TILE), j...  106 us

profile of v3, /device:TPU:1, one launch (start us, length us, event | category | flops | bytes accessed | tf_op | source)
XLA Modules:
  0.0 109.7 jit_solution(8237445366768823233)
XLA Ops:
  1.3 106.3 %shard_map.77.from_ref = bf16[528,4096]{1,0:T(8,128)(2,1)S(1)} custom-call(s32[1,16]{1,0:T(1,128)} %cell_in.1, s32[1,1]{1,0:T(1,128)S(6)} %copy.8.count_in, s32[1,8]{1,0:T(1,128)} %mcol_in.1, s32[1,8]{1,0:T(1,128)} %mlive_in.1, bf16[16,256,256]{2,1,0:T(8,128)(2,1)} %bitcast.3, bf16[8,256,256]{2,1,0:T(8,128)(2,1)} %bitcast.4), custom_call_target="tpu_custom_call" | custom-call | tf_op jit(solution)/shard_map/pallas_call | solution.py:384
  107.6 2.1 %shard_map.78 = (bf16[512,4096]{1,0:T(8,128)(2,1)}, f32[1,1]{1,0:T(1,128)}) custom-call(bf16[528,4096]{1,0:T(8,128)(2,1)S(1)} %shard_map.77.from_ref), custom_call_target="tpu_custom_call" | custom-call | tf_op jit(solution)/shard_map/pallas_call | solution.py:417

commit v4 on v3

--- a/solution.py
+++ b/solution.py
@@ -18,7 +18,7 @@
 DEPTH = 2
 XA, XB, YA, YB = (0, 1), (0, 3), (1, 0), (3, 0)
 NEAR_ROW, NEAR_COL = (1, 3, 4, 12), (2, 6, 1)
-FAR_FIRST = (10, 9, 11, 6, 14, 2, 8, 5, 7, 13, 15, 1, 3, 4, 12)
+CHIPS = 64
 MESH = pl.DeviceIdType.MESH
 
 
@@ -80,8 +80,8 @@
 def kernel(
     cell_in, count_in, mcol_in, mlive_in, f_ref, a_ref, out_ref,
     cell_ref, count_ref, mcol_ref, mlive_ref,
-    a0, a1, a2, a3, a4, a5, a6, a7, fl, fu, s_ref, picked, mb, mm, mb_in, mm_in, tab_v, tab, gains,
-    a_send, a_recv, f_send, f_recv, m_send, m_recv, g_send, g_recv, local_sem,
+    a0, a1, a2, a3, a4, a5, a6, a7, fl, fu, s_ref, picked, mb, mm, mb_in, mm_in, tab_v, tab, pair, gains,
+    a_send, a_recv, f_send, f_recv, m_send, m_recv, g_send, g_recv, plane_sem, local_sem,
 ):
     row, col = lax.axis_index("row"), lax.axis_index("col")
     y, x, z, core = row >> 2, row & 3, col >> 1, col & 1
@@ -299,6 +299,8 @@
             to_scalars.wait()
         if k == 8:
             sib_send(2, 0, 1)
+            for e in (1, 2, 3):
+                pl.semaphore_signal(plane_sem, inc=1, device_id=(row, col ^ (2 * e)), device_id_type=MESH)
         if k == 10:
             for copy in local:
                 copy.wait()
@@ -315,6 +317,7 @@
             total = products(1, total)
             total = products(2, total)
         if k == 12:
+            pl.semaphore_wait(plane_sem, 3)
             sib_send(1, 2, 3)
             sib_send(3, 2, 3)
         if k == 13:
@@ -338,19 +341,33 @@
         return carry
 
     total = jnp.sum(total.reshape(TILE // 64, 8, TILE), axis=0)
-    part = total[:, :128] + total[:, 128:]
-    for k, n in enumerate((N_ROW, N_COL)):
-        gains[k, 0] = part
-        for d in FAR_FIRST if k == 0 else range(n - 1, 0, -1):
-            device = (row, col ^ d) if k else (row ^ d, col)
-            send(gains.at[k, 0], gains.at[k, d], g_send.at[k * N_ROW + d], g_recv.at[k], device)
-        if k == 0:
-            lax.fori_loop(0, 16, output, 0)
-        arrived(gains.at[k, pl.ds(1, n - 1)], g_recv.at[k])
-        parts = [gains[k, d] for d in range(n)]
-        while len(parts) > 1:
-            parts = [parts[2 * i] + parts[2 * i + 1] for i in range(len(parts) // 2)]
-        part = parts[0]
+    pair[0] = total[:, :128] + total[:, 128:]
+    send(pair.at[0], pair.at[1], g_send.at[0], g_recv.at[0], (row, col ^ 1))
+    lax.fori_loop(0, 6, output, 0)
+    arrived(pair.at[1], g_recv.at[0])
+    gains[0] = pair[0] + pair[1]
+    me = (z << 4) | row
+
+    def to_chip(n, carry):
+        @pl.when(n != me)
+        def _():
+            to_row, to_z = n & 15, n >> 4
+            pltpu.make_async_remote_copy(
+                src_ref=gains.at[0], dst_ref=gains.at[((row ^ to_row) << 2) | (z ^ to_z)],
+                send_sem=g_send.at[1], recv_sem=g_recv.at[1],
+                device_id=(to_row, (to_z << 1) | core), device_id_type=MESH,
+            ).start()
+
+        return carry
+
+    lax.fori_loop(0, CHIPS, to_chip, 0, unroll=4)
+    lax.fori_loop(6, 16, output, 0)
+    others = gains.at[pl.ds(1, CHIPS - 1)]
+    arrived(others, g_recv.at[1])
+    part = gains[...]
+    while part.shape[0] > 1:
+        part = part.reshape(part.shape[0] // 2, 2, 8, 128)
+        part = part[:, 0] + part[:, 1]
     rest = jnp.zeros((16, 128), jnp.float32) + jnp.sum(part) * (1.0 / 268435456.0)
     for k in range(3):
         piece = rest.astype(jnp.bfloat16)
@@ -360,6 +377,10 @@
         started.extend(queue)
     for copy in started:
         copy.wait_send()
+    pltpu.make_async_remote_copy(
+        src_ref=others, dst_ref=others, send_sem=g_send.at[1], recv_sem=g_recv.at[1],
+        device_id=(row ^ 1, col), device_id_type=MESH,
+    ).wait_send()
 
 
 def store_kernel(from_ref, to_ref, gain_ref, gain_s, sem):
@@ -399,15 +420,17 @@
             pltpu.VMEM((4, 8, 128), jnp.int32),
             pltpu.VMEM((8, 128), jnp.int32),
             pltpu.SMEM((8, 128), jnp.int32),
-            pltpu.VMEM((2, N_ROW, 8, 128), jnp.float32),
+            pltpu.VMEM((2, 8, 128), jnp.float32),
+            pltpu.VMEM((64, 8, 128), jnp.float32),
             pltpu.SemaphoreType.DMA((60,)),
             pltpu.SemaphoreType.DMA((64,)),
             pltpu.SemaphoreType.DMA((40,)),
             pltpu.SemaphoreType.DMA((48,)),
             pltpu.SemaphoreType.DMA((7,)),
             pltpu.SemaphoreType.DMA((7,)),
-            pltpu.SemaphoreType.DMA((24,)),
             pltpu.SemaphoreType.DMA((2,)),
+            pltpu.SemaphoreType.DMA((2,)),
+            pltpu.SemaphoreType.REGULAR,
             pltpu.SemaphoreType.DMA((9,)),
         ],
         compiler_params=pltpu.CompilerParams(

time: 110 us -> 108 us (0.982)
  Pallas kernels: 108 us -> 106 us
    pallas_call x1, Pallas kernels: 106 us -> 104 us  [on_device(): pl.pallas_call(kernel, out_shape=pltpu.VMEM((2 * TILE + 16, 16 * TILE), j...]
where the time goes in v4:
time: 108 us
  Pallas kernels  106 us (98%)
  between operations  1.28 us (1%)
    pallas_call x1, Pallas kernels, on_device(): pl.pallas_call(kernel, out_shape=pltpu.VMEM((2 * TILE + 16, 16 * TILE), j...  104 us

profile of v4, /device:TPU:1, one launch (start us, length us, event | category | flops | bytes accessed | tf_op | source)
XLA Modules:
  0.0 107.5 jit_solution(5725475598973504377)
XLA Ops:
  1.3 104.2 %shard_map.77.from_ref = bf16[528,4096]{1,0:T(8,128)(2,1)S(1)} custom-call(s32[1,16]{1,0:T(1,128)} %cell_in.1, s32[1,1]{1,0:T(1,128)S(6)} %copy.8.count_in, s32[1,8]{1,0:T(1,128)} %mcol_in.1, s32[1,8]{1,0:T(1,128)} %mlive_in.1, bf16[16,256,256]{2,1,0:T(8,128)(2,1)} %bitcast.3, bf16[8,256,256]{2,1,0:T(8,128)(2,1)} %bitcast.4), custom_call_target="tpu_custom_call" | custom-call | tf_op jit(solution)/shard_map/pallas_call | solution.py:405
  105.5 2.1 %shard_map.78 = (bf16[512,4096]{1,0:T(8,128)(2,1)}, f32[1,1]{1,0:T(1,128)}) custom-call(bf16[528,4096]{1,0:T(8,128)(2,1)S(1)} %shard_map.77.from_ref), custom_call_target="tpu_custom_call" | custom-call | tf_op jit(solution)/shard_map/pallas_call | solution.py:440

commit v5 on v4

--- a/solution.py
+++ b/solution.py
@@ -274,7 +274,8 @@
                 picked[j] = jnp.where(tab[5, LOWER + j] == source, tile, picked[j])
             return carry
 
-        lax.fori_loop(0, 8, upper, 0)
+        if n < 7:
+            lax.fori_loop(0, 8, upper, 0)
         return gain
 
     total = jnp.zeros((TILE // 8, TILE), jnp.float32)
@@ -329,7 +330,9 @@
 
     def spilled(j, gain):
         o = LOWER + j
-        return add_product(o, fu[tab[4, o]], picked[j], gain)
+        a_group, source = group_of(7)
+        tile = jnp.where(tab[5, o] == source, a_group[tab[0, o]], picked[j])
+        return add_product(o, fu[tab[4, o]], tile, gain)
 
     total = lax.fori_loop(0, 8, spilled, total, unroll=UNROLL)
 
@@ -362,21 +365,21 @@
 
     lax.fori_loop(0, CHIPS, to_chip, 0, unroll=4)
     lax.fori_loop(6, 16, output, 0)
+    for queue in flying.values():
+        started.extend(queue)
+    for copy in started:
+        copy.wait_send()
     others = gains.at[pl.ds(1, CHIPS - 1)]
     arrived(others, g_recv.at[1])
     part = gains[...]
     while part.shape[0] > 1:
         part = part.reshape(part.shape[0] // 2, 2, 8, 128)
         part = part[:, 0] + part[:, 1]
-    rest = jnp.zeros((16, 128), jnp.float32) + jnp.sum(part) * (1.0 / 268435456.0)
+    rest = jnp.concatenate([part[0], jnp.zeros((8, 128), jnp.float32)])
     for k in range(3):
         piece = rest.astype(jnp.bfloat16)
         out_ref[pl.ds(2 * TILE, 16), pl.ds(k * 128, 128)] = piece
         rest = rest - piece.astype(jnp.float32)
-    for queue in flying.values():
-        started.extend(queue)
-    for copy in started:
-        copy.wait_send()
     pltpu.make_async_remote_copy(
         src_ref=others, dst_ref=others, send_sem=g_send.at[1], recv_sem=g_recv.at[1],
         device_id=(row ^ 1, col), device_id_type=MESH,
@@ -391,7 +394,7 @@
     gain = jnp.zeros((16, 128), jnp.float32)
     for k in (2, 1, 0):
         gain += from_ref[pl.ds(2 * TILE, 16), pl.ds(k * 128, 128)].astype(jnp.float32)
-    gain_s[0, 0] = gain[0, 0]
+    gain_s[0, 0] = jnp.sum(gain) * (1.0 / 268435456.0)
     copies.append(pltpu.make_async_copy(gain_s, gain_ref, sem.at[4]))
     copies[-1].start()
     for copy in copies:

time: 108 us -> 107 us (level)
  no operation moved by 1% of the time
where the time goes in v5:
time: 107 us
  Pallas kernels  106 us (99%)
  between operations  1.28 us (1%)
    pallas_call x1, Pallas kernels, on_device(): pl.pallas_call(kernel, out_shape=pltpu.VMEM((2 * TILE + 16, 16 * TILE), j...  104 us

profile of v5, /device:TPU:1, one launch (start us, length us, event | category | flops | bytes accessed | tf_op | source)
XLA Modules:
  0.0 107.2 jit_solution(779092527720567522)
XLA Ops:
  1.3 103.9 %shard_map.77.from_ref = bf16[528,4096]{1,0:T(8,128)(2,1)S(1)} custom-call(s32[1,16]{1,0:T(1,128)} %cell_in.1, s32[1,1]{1,0:T(1,128)S(6)} %copy.8.count_in, s32[1,8]{1,0:T(1,128)} %mcol_in.1, s32[1,8]{1,0:T(1,128)} %mlive_in.1, bf16[16,256,256]{2,1,0:T(8,128)(2,1)} %bitcast.3, bf16[8,256,256]{2,1,0:T(8,128)(2,1)} %bitcast.4), custom_call_target="tpu_custom_call" | custom-call | tf_op jit(solution)/shard_map/pallas_call | solution.py:408
  105.2 2.1 %shard_map.78 = (bf16[512,4096]{1,0:T(8,128)(2,1)}, f32[1,1]{1,0:T(1,128)}) custom-call(bf16[528,4096]{1,0:T(8,128)(2,1)S(1)} %shard_map.77.from_ref), custom_call_target="tpu_custom_call" | custom-call | tf_op jit(solution)/shard_map/pallas_call | solution.py:443

commit v6 on v5

--- a/solution.py
+++ b/solution.py
@@ -346,7 +346,7 @@
     total = jnp.sum(total.reshape(TILE // 64, 8, TILE), axis=0)
     pair[0] = total[:, :128] + total[:, 128:]
     send(pair.at[0], pair.at[1], g_send.at[0], g_recv.at[0], (row, col ^ 1))
-    lax.fori_loop(0, 6, output, 0)
+    lax.fori_loop(0, 3, output, 0)
     arrived(pair.at[1], g_recv.at[0])
     gains[0] = pair[0] + pair[1]
     me = (z << 4) | row
@@ -364,7 +364,7 @@
         return carry
 
     lax.fori_loop(0, CHIPS, to_chip, 0, unroll=4)
-    lax.fori_loop(6, 16, output, 0)
+    lax.fori_loop(3, 16, output, 0)
     for queue in flying.values():
         started.extend(queue)
     for copy in started:

time: 107 us -> 107 us (level)
  no operation moved by 1% of the time
where the time goes in v6:
time: 107 us
  Pallas kernels  106 us (99%)
  between operations  1.28 us (1%)
    pallas_call x1, Pallas kernels, on_device(): pl.pallas_call(kernel, out_shape=pltpu.VMEM((2 * TILE + 16, 16 * TILE), j...  104 us

profile of v6, /device:TPU:1, one launch (start us, length us, event | category | flops | bytes accessed | tf_op | source)
XLA Modules:
  0.0 107.3 jit_solution(2215768406033836225)
XLA Ops:
  1.3 104.0 %shard_map.77.from_ref = bf16[528,4096]{1,0:T(8,128)(2,1)S(1)} custom-call(s32[1,16]{1,0:T(1,128)} %cell_in.1, s32[1,1]{1,0:T(1,128)S(6)} %copy.8.count_in, s32[1,8]{1,0:T(1,128)} %mcol_in.1, s32[1,8]{1,0:T(1,128)} %mlive_in.1, bf16[16,256,256]{2,1,0:T(8,128)(2,1)} %bitcast.3, bf16[8,256,256]{2,1,0:T(8,128)(2,1)} %bitcast.4), custom_call_target="tpu_custom_call" | custom-call | tf_op jit(solution)/shard_map/pallas_call | solution.py:408
  105.2 2.1 %shard_map.78 = (bf16[512,4096]{1,0:T(8,128)(2,1)}, f32[1,1]{1,0:T(1,128)}) custom-call(bf16[528,4096]{1,0:T(8,128)(2,1)S(1)} %shard_map.77.from_ref), custom_call_target="tpu_custom_call" | custom-call | tf_op jit(solution)/shard_map/pallas_call | solution.py:443

commit v7 on v5

--- a/solution.py
+++ b/solution.py
@@ -324,9 +324,10 @@
         if k == 13:
             total = products(3, total)
     sib_send(2, 2, 3)
-    for n in range(4, 8):
+    for n in range(4, 7):
         total = products(n, total)
     sib_wait(1)
+    total = products(7, total)
 
     def spilled(j, gain):
         o = LOWER + j

time: 107 us -> 107 us (level)
  no operation moved by 1% of the time
where the time goes in v7:
time: 107 us
  Pallas kernels  106 us (99%)
  between operations  1.28 us (1%)
    pallas_call x1, Pallas kernels, on_device(): pl.pallas_call(kernel, out_shape=pltpu.VMEM((2 * TILE + 16, 16 * TILE), j...  104 us

profile of v7, /device:TPU:1, one launch (start us, length us, event | category | flops | bytes accessed | tf_op | source)
XLA Modules:
  0.0 107.3 jit_solution(2118810458729940869)
XLA Ops:
  1.3 103.9 %shard_map.77.from_ref = bf16[528,4096]{1,0:T(8,128)(2,1)S(1)} custom-call(s32[1,16]{1,0:T(1,128)} %cell_in.1, s32[1,1]{1,0:T(1,128)S(6)} %copy.8.count_in, s32[1,8]{1,0:T(1,128)} %mcol_in.1, s32[1,8]{1,0:T(1,128)} %mlive_in.1, bf16[16,256,256]{2,1,0:T(8,128)(2,1)} %bitcast.3, bf16[8,256,256]{2,1,0:T(8,128)(2,1)} %bitcast.4), custom_call_target="tpu_custom_call" | custom-call | tf_op jit(solution)/shard_map/pallas_call | solution.py:409
  105.2 2.1 %shard_map.78 = (bf16[512,4096]{1,0:T(8,128)(2,1)}, f32[1,1]{1,0:T(1,128)}) custom-call(bf16[528,4096]{1,0:T(8,128)(2,1)S(1)} %shard_map.77.from_ref), custom_call_target="tpu_custom_call" | custom-call | tf_op jit(solution)/shard_map/pallas_call | solution.py:444
